TPU v7x, 512 devices: a whole 4x4x16 slice. The times are simulated.
512 devices in a mesh: dp: 16 (over x, z_hi, core), seq: 32 (over y, z_lo).
Axes of the slice: x: 4, y: 4, z: 16 (z_hi: 2, z_lo: 8; z = z_hi * 8 + z_lo), core: 2. Of those that a mesh axis runs over, the one named last changes fastest.
Arguments:
- latents: bfloat16 [16, 32, 256, 1152], P('dp', 'seq'), may hold values from -5 to 5
- caption: bfloat16 [16, 300, 1152], P('dp'), may hold values from -5 to 5
- caption_len: int32 [16], P('dp'), may hold values from 37 to 300, as said below
- modulation: float32 [16, 3, 1152], P('dp'), may hold values from -1 to 3
- cross_query: bfloat16 [1152, 576], P('seq')
- cross_keyval: bfloat16 [1152, 1152], P('seq')
- cross_output: bfloat16 [576, 1152], P('seq'), may hold values from -0.25 to 0.25
- time_qkv: bfloat16 [1152, 1728], P('seq')
- time_output: bfloat16 [576, 1152], P('seq'), may hold values from -0.25 to 0.25
- cotangent: bfloat16 [16, 32, 256, 1152], P('dp', 'seq'), may hold values from -6 to 6
Outputs:
- output: bfloat16 [16, 32, 256, 1152], P('dp', 'seq')
- grad_latents: bfloat16 [16, 32, 256, 1152], P('dp', 'seq')
- grad_modulation: float32 [16, 3, 1152], P('dp', None, 'seq')
- grad_time_output: float32 [576, 1152], P(None, 'seq')
Inputs may be any that keep to these rules, and one draw needn't show every extreme that they name: `caption_len`: number of caption tokens in use for each clip; the slots from it on are padding.
All inputs are finite; a program needn't handle non-finite values.
Results may differ from a plain program's by a relative error of at most 0.035.
Values may be sent and summed in bfloat16 or wider, within the bound.
A program may use at most 64 MiB of HBM per device.

v0:
```python
import jax
import jax.numpy as jnp
from jax import lax
from jax.sharding import PartitionSpec as P

HEADS = 8


eps_norm = 1e-06
block_rows = 512


def norm_rows(hidden):
    widened = hidden.astype(jnp.float32)
    center = widened - jnp.mean(widened, axis=-1, keepdims=True)
    inv_std = lax.rsqrt(jnp.mean(center * center, axis=-1, keepdims=True) + eps_norm)
    return (center * inv_std, inv_std)


def norm_back(grad_norm, normed, inv_std):
    first_mean = jnp.mean(grad_norm, axis=-1, keepdims=True)
    second_mean = jnp.mean(grad_norm * normed, axis=-1, keepdims=True)
    return inv_std * (grad_norm - first_mean - normed * second_mean)


def relayout(blocks):
    return lax.all_to_all(blocks, "seq", split_axis=1, concat_axis=0, tiled=True)


def to_patches(frame_rows, frames_dev, patch_count):
    seq_parts = lax.axis_size("seq")
    grid = frame_rows.reshape(frames_dev, seq_parts, patch_count // seq_parts, frame_rows.shape[1])
    return relayout(grid).reshape(-1, frame_rows.shape[1])


def to_frames(patch_rows, frames_all):
    grid = patch_rows.reshape(1, frames_all, -1, patch_rows.shape[1])
    moved = relayout(grid)
    return jnp.swapaxes(moved, 0, 1).reshape(-1, patch_rows.shape[1])


def cross_soft(query_block, key_rows, length, head_scale):
    scores = (
        jnp.einsum("rhe,che->hrc", query_block, key_rows, preferred_element_type=jnp.float32)
        * head_scale
    )
    valid = jnp.arange(key_rows.shape[0], dtype=jnp.int32) < length
    return jax.nn.softmax(jnp.where(valid, scores, -1e30), axis=-1)


def split_heads(packed, index, inner_width):
    block = packed[..., index * inner_width : (index + 1) * inner_width]
    return block.reshape(block.shape[:-1] + (HEADS, inner_width // HEADS))


def time_soft(packed, inner_width):
    queries = split_heads(packed, 0, inner_width)
    key_rows = split_heads(packed, 1, inner_width)
    head_scale = (inner_width // HEADS) ** (-0.5)
    scores = (
        jnp.einsum("fphe,gphe->phfg", queries, key_rows, preferred_element_type=jnp.float32)
        * head_scale
    )
    return (jax.nn.softmax(scores, axis=-1), queries, key_rows)


def time_forward(packed, inner_width):
    soft, queries, key_rows = time_soft(packed, inner_width)
    value_rows = split_heads(packed, 2, inner_width)
    mixed = jnp.einsum(
        "phfg,gphe->fphe", soft.astype(jnp.bfloat16), value_rows, preferred_element_type=jnp.float32
    )
    return mixed.reshape(mixed.shape[:2] + (inner_width,)).astype(jnp.bfloat16)


def time_backward(packed, grad_mixed, inner_width):
    soft, queries, key_rows = time_soft(packed, inner_width)
    value_rows = split_heads(packed, 2, inner_width)
    head_scale = (inner_width // HEADS) ** (-0.5)
    grad_heads = grad_mixed.reshape(grad_mixed.shape[:2] + (HEADS, inner_width // HEADS))
    grad_soft = jnp.einsum(
        "fphe,gphe->phfg", grad_heads, value_rows, preferred_element_type=jnp.float32
    )
    grad_values = jnp.einsum(
        "phfg,fphe->gphe", soft.astype(jnp.bfloat16), grad_heads, preferred_element_type=jnp.float32
    ).astype(jnp.bfloat16)
    delta_rows = jnp.sum(soft * grad_soft, axis=-1, keepdims=True)
    grad_scores = (soft * (grad_soft - delta_rows) * head_scale).astype(jnp.bfloat16)
    grad_queries = jnp.einsum(
        "phfg,gphe->fphe", grad_scores, key_rows, preferred_element_type=jnp.float32
    ).astype(jnp.bfloat16)
    grad_keys = jnp.einsum(
        "phfg,fphe->gphe", grad_scores, queries, preferred_element_type=jnp.float32
    ).astype(jnp.bfloat16)
    lead = grad_mixed.shape[:2] + (inner_width,)
    return jnp.concatenate(
        [grad_queries.reshape(lead), grad_keys.reshape(lead), grad_values.reshape(lead)], axis=-1
    )


def body(
    latents,
    caption,
    caption_len,
    modulation,
    cross_query,
    cross_keyval,
    cross_output,
    time_qkv,
    time_output,
    cotangent,
):
    frames_dev = latents.shape[1]
    patch_count = latents.shape[2]
    model_width = latents.shape[3]
    frames_all = frames_dev * lax.axis_size("seq")
    row_count = frames_dev * patch_count
    inner_width = cross_query.shape[1]
    head_size = inner_width // HEADS
    head_scale = head_size ** (-0.5)
    caption_rows = caption[0]
    length = caption_len[0]
    shift_row = modulation[0, 0]
    scale_row = modulation[0, 1]
    gate_row = modulation[0, 2]
    query_full, cross_out_full, qkv_full, time_out_full, keyval_full = (
        lax.all_gather(cross_query, "seq", axis=0, tiled=True),
        lax.all_gather(cross_output, "seq", axis=0, tiled=True),
        lax.all_gather(time_qkv, "seq", axis=0, tiled=True),
        lax.all_gather(time_output, "seq", axis=0, tiled=True),
        lax.all_gather(cross_keyval, "seq", axis=0, tiled=True),
    )
    keyval = jnp.dot(caption_rows, keyval_full, preferred_element_type=jnp.float32).astype(
        jnp.bfloat16
    )
    key_rows = keyval[:, :inner_width].reshape(-1, HEADS, head_size)
    value_rows = keyval[:, inner_width:].reshape(-1, HEADS, head_size)
    latent_rows = latents.reshape(row_count, model_width)
    queries = jnp.dot(latent_rows, query_full, preferred_element_type=jnp.float32).astype(
        jnp.bfloat16
    )
    block_size = min(block_rows, row_count)
    block_count = row_count // block_size
    query_blocks = queries.reshape(block_count, block_size, HEADS, head_size)

    def attend_block(query_block):
        soft = cross_soft(query_block, key_rows, length, head_scale)
        mixed = jnp.einsum(
            "hrc,che->rhe",
            soft.astype(jnp.bfloat16),
            value_rows,
            preferred_element_type=jnp.float32,
        )
        return mixed.astype(jnp.bfloat16)

    attended = lax.map(attend_block, query_blocks).reshape(row_count, inner_width)
    hidden = (
        latent_rows.astype(jnp.float32)
        + jnp.dot(attended, cross_out_full, preferred_element_type=jnp.float32)
    ).astype(jnp.bfloat16)
    hidden_patch = to_patches(hidden, frames_dev, patch_count)
    normed, inv_std = norm_rows(hidden_patch)
    modded = (normed * (1.0 + scale_row) + shift_row).astype(jnp.bfloat16)
    normed, inv_std, modded = (normed, inv_std, modded)
    packed = jnp.dot(modded, qkv_full, preferred_element_type=jnp.float32).astype(jnp.bfloat16)
    packed = packed.reshape(frames_all, -1, 3 * inner_width)
    mixed = time_forward(packed, inner_width).reshape(-1, inner_width)
    branch = jnp.dot(mixed, time_out_full, preferred_element_type=jnp.float32)
    output_patch = (hidden_patch.astype(jnp.float32) + gate_row * branch).astype(jnp.bfloat16)
    output_rows = to_frames(output_patch, frames_all)
    grad_rows = to_patches(
        cotangent.reshape(row_count, model_width), frames_dev, patch_count
    ).astype(jnp.float32)
    grad_branch = (gate_row * grad_rows).astype(jnp.bfloat16)
    grad_gate = jnp.sum(grad_rows * branch, axis=0)
    grad_weight = jnp.einsum("ri,rd->id", mixed, grad_branch, preferred_element_type=jnp.float32)
    grad_mixed = jnp.einsum(
        "rd,id->ri", grad_branch, time_out_full, preferred_element_type=jnp.float32
    ).astype(jnp.bfloat16)
    grad_gate, grad_weight, grad_mixed = (grad_gate, grad_weight, grad_mixed)
    grad_packed = time_backward(
        packed, grad_mixed.reshape(frames_all, -1, inner_width), inner_width
    )
    grad_packed = grad_packed.reshape(-1, 3 * inner_width)
    grad_modded = jnp.einsum("rk,dk->rd", grad_packed, qkv_full, preferred_element_type=jnp.float32)
    grad_shift = jnp.sum(grad_modded, axis=0)
    grad_scale = jnp.sum(grad_modded * normed, axis=0)
    term = norm_back(grad_modded * (1.0 + scale_row), normed, inv_std).astype(jnp.bfloat16)
    grad_shift, grad_scale, term = (grad_shift, grad_scale, term)
    grad_hidden = to_frames((grad_rows + term.astype(jnp.float32)).astype(jnp.bfloat16), frames_all)
    grad_attended = jnp.einsum(
        "rd,id->ri", grad_hidden, cross_out_full, preferred_element_type=jnp.float32
    ).astype(jnp.bfloat16)

    def back_block(pair):
        query_block, grad_block = pair
        soft = cross_soft(query_block, key_rows, length, head_scale)
        grad_soft = jnp.einsum(
            "rhe,che->hrc", grad_block, value_rows, preferred_element_type=jnp.float32
        )
        delta_rows = jnp.sum(soft * grad_soft, axis=-1, keepdims=True)
        grad_score = (soft * (grad_soft - delta_rows) * head_scale).astype(jnp.bfloat16)
        return jnp.einsum(
            "hrc,che->rhe", grad_score, key_rows, preferred_element_type=jnp.float32
        ).astype(jnp.bfloat16)

    grad_blocks = grad_attended.reshape(block_count, block_size, HEADS, head_size)
    grad_queries = lax.map(back_block, (query_blocks, grad_blocks)).reshape(row_count, inner_width)
    grad_input = grad_hidden.astype(jnp.float32) + jnp.einsum(
        "ri,di->rd", grad_queries, query_full, preferred_element_type=jnp.float32
    )
    grad_input = grad_input.astype(jnp.bfloat16)
    per_clip = frames_all * patch_count
    total_tokens = per_clip * lax.axis_size("dp")
    mod_part = jnp.stack([grad_shift, grad_scale, grad_gate])
    weight_share, mod_share = (
        lax.psum_scatter(grad_weight, "seq", scatter_dimension=1, tiled=True),
        lax.psum_scatter(mod_part, "seq", scatter_dimension=1, tiled=True),
    )
    weight_total = lax.psum(weight_share, "dp") * total_tokens ** (-0.5)
    mod_out = (mod_share * per_clip ** (-0.5)).reshape(1, 3, -1)
    return (
        output_rows.reshape(latents.shape),
        grad_input.reshape(latents.shape),
        mod_out,
        weight_total,
    )


def solution(mesh):
    placed = (
        P("dp", "seq", None, None),
        P("dp", None, None),
        P("dp"),
        P("dp", None, None),
        P("seq", None),
        P("seq", None),
        P("seq", None),
        P("seq", None),
        P("seq", None),
        P("dp", "seq", None, None),
    )
    return jax.shard_map(
        body,
        mesh=mesh,
        in_specs=placed,
        out_specs=(
            P("dp", "seq", None, None),
            P("dp", "seq", None, None),
            P("dp", None, "seq"),
            P(None, "seq"),
        ),
        check_vma=False,
    )
```

profile of v0, /device:TPU:1, one launch (start us, length us, event | category | flops | bytes accessed | tf_op | source)
XLA Modules:
  0.0 1957.1 jit_solution(9688630853324500625)
XLA Ops:
  10.6 16.2 all-to-all-start.2
  27.5 194.0 %all-gather.13.cloned.1.call-done = bf16[32,36,576]{2,1,0:T(8,128)(2,1)} async-done(((bf16[1,36,576]{2,1,0:T(8,128)(2,1)}), bf16[32,36,576]{2,1,0:T(8,128)(2,1)}) %all-gather.13.cloned.1.call-update) | async-done | bytes 1327120 | tf_op jit(solution)/shard_map/all_gather | solution.py:127
  224.0 222.6 %all-gather.15.cloned.1.call-done = bf16[32,18,1152]{2,1,0:T(8,128)(2,1)} async-done(((bf16[1,18,1152]{2,1,0:T(8,128)(2,1)}), bf16[32,18,1152]{2,1,0:T(8,128)(2,1)}) %all-gather.15.cloned.1.call-update) | async-done | bytes 1327120 | tf_op jit(solution)/shard_map/all_gather | solution.py:128
  451.9 227.6 %all-gather.11.cloned.1.call-done = bf16[32,36,1152]{2,1,0:T(8,128)(2,1)} async-done(((bf16[1,36,1152]{2,1,0:T(8,128)(2,1)}), bf16[32,36,1152]{2,1,0:T(8,128)(2,1)}) %all-gather.11.cloned.1.call-update) | async-done | bytes 2654224 | tf_op jit(solution)/shard_map/all_gather | solution.py:131
  679.5 5.2 reshape.198
  692.5 3.6 fusion.120
  700.1 9.4 all-to-all-start
  709.5 194.4 %all-gather.19.cloned.1.call-done = bf16[32,18,1152]{2,1,0:T(8,128)(2,1)} async-done(((bf16[1,18,1152]{2,1,0:T(8,128)(2,1)}), bf16[32,18,1152]{2,1,0:T(8,128)(2,1)}) %all-gather.19.cloned.1.call-update) | async-done | bytes 1327120 | tf_op jit(solution)/shard_map/all_gather | solution.py:130
  912.6 231.6 %all-gather.17.cloned.1.call-done = bf16[32,36,1728]{2,1,0:T(8,128)(2,1)} async-done(((bf16[1,36,1728]{2,1,0:T(8,128)(2,1)}), bf16[32,36,1728]{2,1,0:T(8,128)(2,1)}) %all-gather.17.cloned.1.call-update) | async-done | bytes 3981328 | tf_op jit(solution)/shard_map/all_gather | solution.py:129
  1144.2 7.3 reshape.204
  1151.5 5.0 convolution_convert_fusion.1
  1174.1 4.0 fusion.34
  1178.1 4.0 fusion.35
  1196.7 4.2 fusion.58
  1204.1 8.2 all-to-all-start.1
  1215.6 17.8 all-to-all-done.1
  1233.5 4.6 all-to-all-start.3
  1238.1 139.1 %fusion = f32[576,48]{0,1:T(8,128)} fusion(f32[576,1152]{0,1:T(8,128)} %fusion.71), kind=kCustom, calls=%all-reduce-scatter | all-reduce-scatter fusion | flops 884737 | bytes 2766848
  1385.9 6.4 collective-permute-start.3
  1394.3 7.4 collective-permute-start.1
  1404.9 197.3 %all-reduce = f32[3,1152]{1,0:T(4,128)S(1)} all-reduce(f32[3,1152]{1,0:T(4,128)S(1)} %pad_maximum_fusion), channel_id=2, replica_groups=mesh['dp'=16,'seq'=32] {'seq'}, use_global_device_ids=true, to_apply=%region_13.14.clone | all-reduce | flops 3456 | bytes 27648
  1602.3 14.3 concatenate.14
  1618.8 317.9 %all-reduce.5.cloned.1.call-done = f32[576,36]{0,1:T(8,128)} async-done(((f32[576,36]{0,1:T(8,128)}), f32[576,36]{0,1:T(8,128)}) %all-reduce.5.cloned.1.call-update) | async-done | bytes 82960 | tf_op jit(solution)/shard_map/psum | solution.py:220
  1942.0 4.8 fusion.37
  (121 shorter events, 93.6 us)
Async XLA Ops:
  7.2 677.5 %copy-start = (bf16[1,300,1152]{2,1,0:T(8,128)(2,1)S(1)}, bf16[1,300,1152]{2,1,0:T(8,128)(2,1)}, u32[]{:S(2)}) copy-start(bf16[1,300,1152]{2,1,0:T(8,128)(2,1)} %param.11) | copy-start | bytes 2073604
  7.2 214.2 %all-gather.13.cloned.1.call-start = ((), (), s32[]{:S(2)}) async-start(), calls=%async_computation.6 | async-start | bytes 1689600 | tf_op jit(solution)/shard_map/all_gather | solution.py:127
  7.9 438.7 %all-gather.15.cloned.1.call-start = ((), (), s32[]{:S(2)}) async-start(), calls=%async_computation.7 | async-start | bytes 1824768 | tf_op jit(solution)/shard_map/all_gather | solution.py:128
  8.7 670.9 %all-gather.11.cloned.1.call-start = ((), (), s32[]{:S(2)}) async-start(), calls=%async_computation.5 | async-start | bytes 3041280 | tf_op jit(solution)/shard_map/all_gather | solution.py:131
  9.4 894.5 %all-gather.19.cloned.1.call-start = ((), (), s32[]{:S(2)}) async-start(), calls=%async_computation.9 | async-start | bytes 1824768 | tf_op jit(solution)/shard_map/all_gather | solution.py:130
  10.0 1134.2 %all-gather.17.cloned.1.call-start = ((), (), s32[]{:S(2)}) async-start(), calls=%async_computation.8 | async-start | bytes 4730880 | tf_op jit(solution)/shard_map/all_gather | solution.py:129
  10.6 689.5 %all-to-all-start.2 = ((bf16[1,32,8,1152]{3,2,0,1:T(8,128)(2,1)}), bf16[1,32,8,1152]{3,2,0,1:T(8,128)(2,1)}, u32[]{:S(2)}, u32[]{:S(2)}) async-start(bf16[1,32,8,1152]{3,2,0,1:T(8,128)(2,1)} %bitcast.151), calls=%async_computation.2 | async-start | bytes 1179648 | tf_op jit(solution)/shard_map/all_to_all | solution.py:27
  449.0 249.5 %copy-start.1 = (bf16[576,1152]{1,0:T(8,128)(2,1)}, bf16[576,1152]{1,0:T(8,128)(2,1)S(1)}, u32[]{:S(2)}) copy-start(bf16[576,1152]{1,0:T(8,128)(2,1)S(1)} %reshape.202) | copy-start | bytes 3981316
  700.1 211.9 %all-to-all-start = ((bf16[1,32,8,1152]{3,2,0,1:T(8,128)(2,1)}), bf16[1,32,8,1152]{3,2,0,1:T(8,128)(2,1)S(1)}, u32[]{:S(2)}, u32[]{:S(2)}) async-start(bf16[1,32,8,1152]{3,2,0,1:T(8,128)(2,1)} %fusion.9), calls=%async_computation | async-start | bytes 1179648 | tf_op jit(solution)/shard_map/all_to_all | solution.py:27
  1204.1 29.3 %all-to-all-start.1 = ((bf16[1,32,8,1152]{3,2,0,1:T(8,128)(2,1)}), bf16[1,32,8,1152]{3,2,0,1:T(8,128)(2,1)S(1)}, u32[]{:S(2)}, u32[]{:S(2)}) async-start(bf16[1,32,8,1152]{3,2,0,1:T(8,128)(2,1)} %get-tuple-element.63), calls=%async_computation.1 | async-start | bytes 1179648 | tf_op jit(solution)/shard_map/all_to_all | solution.py:27
  1233.5 143.8 %copy-start.3 = (bf16[1,32,8,1152]{3,2,0,1:T(8,128)(2,1)}, bf16[1,32,8,1152]{3,2,0,1:T(8,128)(2,1)S(1)}, u32[]{:S(2)}) copy-start(bf16[1,32,8,1152]{3,2,0,1:T(8,128)(2,1)S(1)} %all-to-all-done.1) | copy-start | bytes 1769476
  1233.5 704.8 %all-to-all-start.3 = ((bf16[1,32,8,1152]{3,2,0,1:T(8,128)(2,1)}), bf16[1,32,8,1152]{3,2,0,1:T(8,128)(2,1)}, u32[]{:S(2)}, u32[]{:S(2)}) async-start(bf16[1,32,8,1152]{3,2,0,1:T(8,128)(2,1)} %get-tuple-element.64), calls=%async_computation.3 | async-start | bytes 1179648 | tf_op jit(solution)/shard_map/all_to_all | solution.py:27
  1238.1 144.0 %copy-start.16 = (u32[512]{0:T(512)S(1)}, u32[512]{0:T(512)}, u32[]{:S(2)}) copy-start(u32[512]{0:T(512)} %constant.69) | copy-start | bytes 6148
  1238.1 698.6 %all-reduce.5.cloned.1.call-start = ((), (), s32[]{:S(2)}) async-start(), calls=%async_computation.4 | async-start | bytes 204800 | tf_op jit(solution)/shard_map/psum | solution.py:220
  1377.2 17.1 collective-permute-start.6
  1378.5 23.2 %collective-permute-start.5 = (f32[576,48]{0,1:T(8,128)}, f32[576,48]{0,1:T(8,128)S(1)}, u32[]{:S(2)}, u32[]{:S(2)}) collective-permute-start(f32[576,48]{0,1:T(8,128)} %fusion), channel_id=1, source_target_pairs={{0,6},{1,7},{2,8},{3,9},{4,10},{5,11},{6,12},{7,13},{8,14},{9,15},... | collective-permute-start | bytes 331784
  1380.7 11.6 collective-permute-start.7
  1384.0 218.3 %collective-permute-start.4 = (f32[576,48]{0,1:T(8,128)}, f32[576,48]{0,1:T(8,128)}, u32[]{:S(2)}, u32[]{:S(2)}) collective-permute-start(f32[576,48]{0,1:T(8,128)} %fusion), channel_id=1, source_target_pairs={{0,5},{1,6},{2,7},{3,8},{4,9},{5,10},{6,11},{7,12},{8,13},{9,14},{... | collective-permute-start | bytes 331784
  1385.9 216.4 %collective-permute-start.3 = (f32[576,48]{0,1:T(8,128)}, f32[576,48]{0,1:T(8,128)}, u32[]{:S(2)}, u32[]{:S(2)}) collective-permute-start(f32[576,48]{0,1:T(8,128)} %fusion), channel_id=1, source_target_pairs={{0,4},{1,5},{2,6},{3,7},{4,8},{5,9},{6,10},{7,11},{8,12},{9,13},{1... | collective-permute-start | bytes 331784
  1392.4 12.5 copy-start.14
  1392.4 209.9 %collective-permute-start.2 = (f32[576,48]{0,1:T(8,128)}, f32[576,48]{0,1:T(8,128)}, u32[]{:S(2)}, u32[]{:S(2)}) collective-permute-start(f32[576,48]{0,1:T(8,128)} %fusion), channel_id=1, source_target_pairs={{0,3},{1,4},{2,5},{3,6},{4,7},{5,8},{6,9},{7,10},{8,11},{9,12},{10... | collective-permute-start | bytes 331784
  1394.3 207.9 %collective-permute-start.1 = (f32[576,48]{0,1:T(8,128)}, f32[576,48]{0,1:T(8,128)}, u32[]{:S(2)}, u32[]{:S(2)}) collective-permute-start(f32[576,48]{0,1:T(8,128)} %fusion), channel_id=1, source_target_pairs={{0,2},{1,3},{2,4},{3,5},{4,6},{5,7},{6,8},{7,9},{8,10},{9,11},{10,... | collective-permute-start | bytes 331784
  1401.8 200.5 %collective-permute-start = (f32[576,48]{0,1:T(8,128)}, f32[576,48]{0,1:T(8,128)}, u32[]{:S(2)}, u32[]{:S(2)}) collective-permute-start(f32[576,48]{0,1:T(8,128)} %fusion), channel_id=1, source_target_pairs={{0,1},{1,2},{2,3},{3,4},{4,5},{5,6},{6,7},{7,8},{8,9},{9,10},{10,1... | collective-permute-start | bytes 331784
  1602.3 336.0 %copy-start.2 = (bf16[576,1152]{1,0:T(8,128)(2,1)S(1)}, bf16[576,1152]{1,0:T(8,128)(2,1)}, u32[]{:S(2)}) copy-start(bf16[576,1152]{1,0:T(8,128)(2,1)} %copy-done.1) | copy-start | bytes 3981316
  (12 other events, 48.4 us)
Sparse Core Ops, SparseCore 0:
  10.1 211.2 all-gather.12
  223.5 223.0 all-gather.14
  448.7 230.7 all-gather.10
  681.5 222.4 all-gather.18
  905.9 238.2 all-gather.16
  1618.3 318.3 all-reduce.4
where the time goes:
time: 1960 us
  waiting for transfers between devices  1410 us (72%)
  blocking collectives  336 us (17%)
  local copies, waits for them, and re-layouts  69.2 us (4%)
  starting transfers between devices  63.4 us (3%)
  matrix products  60.5 us (3%)
    unnamed x2, blocking collectives  336 us
    psum x1, waiting for transfers between devices, body(): weight_total = lax.psum(weight_share, 'dp') * total_tokens ** (-0.5)  318 us
    all_gather x1, waiting for transfers between devices, body(): lax.all_gather(time_qkv, 'seq', axis=0, tiled=True)  232 us
    all_gather x1, waiting for transfers between devices, body(): lax.all_gather(cross_keyval, 'seq', axis=0, tiled=True)  228 us
    all_gather x1, waiting for transfers between devices, body(): lax.all_gather(cross_output, 'seq', axis=0, tiled=True)  223 us
    all_gather x1, waiting for transfers between devices, body(): lax.all_gather(time_output, 'seq', axis=0, tiled=True)  194 us
    all_gather x1, waiting for transfers between devices, body(): lax.all_gather(cross_query, 'seq', axis=0, tiled=True)  194 us
    unnamed x47, local copies, waits for them, and re-layouts  39.7 us
  transfers between devices with their start and end apart: 18, of which 7 were waited for; matrix products, arithmetic and copies ran while one was open for 10% of the time, Pallas kernels for 0%

commit v1 on v0

v1 whole, which is shorter than its diff:
```python
import jax
import jax.numpy as jnp
from jax import lax
from jax.experimental import pallas as pl
from jax.experimental.pallas import tpu as pltpu
from jax.sharding import PartitionSpec as P

MESH = pl.DeviceIdType.MESH
F32 = jnp.float32
BF16 = jnp.bfloat16
HEADS = 8
HEAD = 72
INNER = HEADS * HEAD
WIDE = 640
MODEL = 1152
ROWS = 256
SLOTS = 384
SEQ = 32
EPS = 1e-6
NEG = -1e30
HEAD_SCALE = HEAD ** (-0.5)
RB, R0, R1, RM, R2 = range(5)
STAGED = {R0: 0, R1: 288, RM: 576, RB: 864, R2: 1008}
FIRST_BLOCK = {RB: 0, R0: 0, R1: 8, R2: 16, RM: 24}


def dot_nn(a, b):
    return lax.dot_general(a, b, (((1,), (0,)), ((), ())), preferred_element_type=F32)


def dot_nt(a, b):
    return lax.dot_general(a, b, (((1,), (1,)), ((), ())), preferred_element_type=F32)


def dot_tn(a, b):
    return lax.dot_general(a, b, (((0,), (0,)), ((), ())), preferred_element_type=F32)


def window(head):
    low = HEAD * head // 128 * 128
    high = -(-(HEAD * (head + 1)) // 128) * 128
    return low, high


def head_mask(head):
    low, high = window(head)
    lane = lax.broadcasted_iota(jnp.int32, (1, high - low), 1) + low
    return jnp.where((lane >= HEAD * head) & (lane < HEAD * (head + 1)), 1.0, 0.0).astype(BF16)


def kernel(
    query_shard,
    keyval_shard,
    cross_out_shard,
    qkv_shard,
    time_out_shard,
    latents,
    caption,
    length_ref,
    modulation,
    cotangent,
    out_ref,
    grad_latents,
    grad_mod,
    grad_weight,
    cols_a,
    cols_b,
    qkv_wide,
    pair_rows,
    z_wide_send,
    z_send,
    z_recv,
    z_wide,
    z_rows,
    own,
    keyval_wide,
    latent_rows,
    rows_wide,
    latent_recv,
    att_send,
    att_recv,
    wa,
    wb,
    cross_out,
    time_out,
    keys,
    values,
    queries,
    probs_c,
    acc,
    hidden_rows,
    gm_send,
    gm_recv,
    mix_send,
    mix_recv,
    term_send,
    term_recv,
    normed_ref,
    packed_ref,
    probs_t,
    grad_branch,
    gw_send,
    gw_core,
    gw_half,
    gw_x,
    gw_part,
    gw_y1,
    gw_part1,
    gw_y,
    gw_tile,
    gw_z,
    gw_red,
    gw_all,
    gw_last,
    mod_sum,
    mod_y,
    mod_tile,
    mod_z,
    zs_send,
    zs_recv,
    ring_send,
    a_recv,
    b_recv,
    core_send,
    core_recv,
    local_sem,
    all_send,
    all_recv,
    red_send,
    red_recv,
    core_part_recv,
):
    dp, s = lax.axis_index("dp"), lax.axis_index("seq")
    x, zh, c = dp // 4, (dp // 2) % 2, dp % 2
    y, zl = s // 8, s % 8
    z = zh * 8 + zl
    u = c * 4 + x

    def at(px, py, pz, pc):
        px, py, pz = lax.rem(px + 4, 4), lax.rem(py + 4, 4), lax.rem(pz + 16, 16)
        return (px * 4 + (pz // 8) * 2 + pc, py * 8 + lax.rem(pz, 8))

    def remote(src, dst, send, recv, device):
        return pltpu.make_async_remote_copy(
            src_ref=src, dst_ref=dst, send_sem=send, recv_sem=recv, device_id=device, device_id_type=MESH
        )

    def wait_bytes(ref, sem):
        pltpu.make_async_copy(ref, ref, sem).wait()

    barrier = pltpu.get_barrier_semaphore()

    def greet(i, carry):
        pl.semaphore_signal(barrier, inc=1, device_id=(dp, lax.rem(s + i, SEQ)), device_id_type=MESH)
        return carry

    lax.fori_loop(1, SEQ, greet, 0)
    for i in range(8):
        pl.semaphore_signal(barrier, inc=1, device_id=at(x, y, (1 - zh) * 8 + i, c), device_id_type=MESH)
    for i in range(1, 8):
        peer = lax.rem(x * 2 + c + i, 8)
        pl.semaphore_signal(barrier, inc=1, device_id=at(peer // 2, y, z, peer % 2), device_id_type=MESH)

    cols_a[...] = jnp.zeros_like(cols_a)
    qkv_wide[...] = jnp.zeros_like(qkv_wide)
    z_wide_send[...] = jnp.zeros_like(z_wide_send)
    cols_a[0:36, 0:1152] = keyval_shard[...].astype(F32)
    cols_a[0:36, 1152:1728] = query_shard[...].astype(F32)
    qkv_wide[0:36, 0:1728] = qkv_shard[...].astype(F32)
    turned = pltpu.roll(qkv_wide[...], 64, 1)
    cols_a[:, 1664:1792] += turned[:, 0:128]
    cols_a[:, 1792:3456] = turned[:, 128:1792]
    cols_b[0:18, 0:128] = time_out_shard[:, 1024:1152].astype(F32)
    cols_b[0:18, 128:1280] = cross_out_shard[...].astype(F32)
    cols_b[0:18, 1280:2304] = time_out_shard[:, 0:1024].astype(F32)

    def block_of(first):
        return pl.ds(pl.multiple_of(first * 128, 128), 128)

    z_wide_send[0:36, :] = cols_a[0:36, block_of(u)]
    z_wide_send[36:72, :] = cols_a[0:36, block_of(8 + u)]
    z_wide_send[128:164, :] = cols_a[0:36, block_of(16 + u)]
    z_wide_send[108:126, :] = cols_b[0:18, block_of(10 + u)]
    pair = lax.max(u - 3, 0)
    pair_rows[0:18, :] = cols_b[0:18, block_of(2 * pair)]
    pair_rows[18:36, :] = cols_b[0:18, block_of(2 * pair + 1)]
    z_wide_send[72:108, :] = jnp.where(u < 3, cols_a[0:36, block_of(lax.min(24 + u, 26))], pair_rows[0:36, :])
    z_send[...] = z_wide_send[...].astype(BF16)

    pl.semaphore_wait(barrier, 31 + 8 + 7)

    def along_z(part, first, count, step):
        rows = pl.ds(first, count)
        remote(
            z_send.at[rows], z_recv.at[zl, rows], zs_send.at[part], zs_recv.at[part], at(x, y, z + step, c)
        ).start()

    for part, first, cut, count in ((0, 0, 64, 128), (1, 128, 32, 48)):
        for step in (1, -1, 2, -2, 3, -3):
            along_z(part, first, count, step)
        along_z(part, first, cut, 4)
        along_z(part, first + cut, count - cut, -4)
    z_recv[pl.ds(zl, 1)] = z_send[...].reshape(1, 176, 128)

    shift_row = modulation[0]
    scale_row = 1.0 + modulation[1]
    gate_row = modulation[2]
    grad_branch[...] = (gate_row * cotangent[...].astype(F32)).astype(BF16)
    latent_rows[...] = latents[...].astype(F32).reshape(ROWS, MODEL).astype(BF16)
    keys[...] = jnp.zeros_like(keys)
    values[...] = jnp.zeros_like(values)
    keyval_wide[296:304, :] = jnp.zeros((8, MODEL), F32)
    rows_wide[...] = jnp.zeros_like(rows_wide)
    cross_out[INNER:WIDE, :] = jnp.zeros((WIDE - INNER, MODEL), BF16)
    time_out[INNER:WIDE, :] = jnp.zeros((WIDE - INNER, MODEL), BF16)
    mod_sum[...] = jnp.zeros_like(mod_sum)

    def place(i, j):
        px = lax.rem(x + i * (1 - c) + j * c + 4, 4)
        py = lax.rem(y + i * c + j * (1 - c) + 4, 4)
        return px, py

    def neighbour(i, j):
        px, py = place(i, j)
        return at(px, py, z, c)

    def piece(k, i, j, half=None):
        px, py = place(i, j)
        count = 144 if k == RB else 288
        start, size = 0, count
        if half is not None:
            cut = 80 if k == RB else 144
            start, size = (0, cut) if half == 0 else (cut, count - cut)
        buf = wb if k == RB else wa
        row = pl.multiple_of(py * count + start, 16)
        col = pl.multiple_of((FIRST_BLOCK[k] + 4 * c + px) * 128, 128)
        return buf.at[pl.ds(row, size), pl.ds(col, 128)]

    def own_piece(k):
        return own.at[pl.ds(STAGED[k], 144 if k == RB else 288)]

    def pieces_like(k, count):
        return wa.at[pl.ds(0, 144 if k == RB else 288), pl.ds(0, 128 * count)]

    def halves_like(k, half, count):
        size = (80 if half == 0 else 64) if k == RB else 144
        return wa.at[pl.ds(0, size), pl.ds(0, 128 * count)]

    def core_part(k, core):
        buf = wb if k == RB else wa
        col = pl.multiple_of((FIRST_BLOCK[k] + 4 * core) * 128, 128)
        return buf.at[:, pl.ds(col, 512)]

    def stage1(k):
        pltpu.make_async_copy(own_piece(k), piece(k, 0, 0), local_sem.at[k]).start()
        for side, step in ((0, 1), (1, -1)):
            remote(own_piece(k), piece(k, 0, 0), ring_send.at[k], a_recv.at[k, side], neighbour(step, 0)).start()

    def stage2(k):
        for side, step in ((0, 1), (1, -1)):
            wait_bytes(piece(k, -step, 0), a_recv.at[k, side])
            ref = piece(k, -step, 0, half=side)
            remote(ref, ref, ring_send.at[k], a_recv.at[k, 2 + side], neighbour(step, 0)).start()
        for i in (0, -1, 1):
            for side, step in ((0, 1), (1, -1)):
                src = own_piece(k) if i == 0 else piece(k, i, 0)
                remote(src, piece(k, i, 0), ring_send.at[k], b_recv.at[k, side], neighbour(0, step)).start()

    def stage3(k):
        for side in (0, 1):
            wait_bytes(halves_like(k, side, 1), a_recv.at[k, 2 + side])
        for side, step in ((0, 1), (1, -1)):
            ref = piece(k, 2, 0)
            remote(ref, ref, ring_send.at[k], b_recv.at[k, side], neighbour(0, step)).start()
        pltpu.make_async_copy(own_piece(k), piece(k, 0, 0), local_sem.at[k]).wait()
        to_core(k, [(i, 0) for i in (0, -1, 1, 2)])

    def stage4(k):
        for side, step in ((0, 1), (1, -1)):
            wait_bytes(pieces_like(k, 4), b_recv.at[k, side])
            for i in (0, -1, 1, 2):
                ref = piece(k, i, -step, half=side)
                remote(ref, ref, ring_send.at[k], b_recv.at[k, 2 + side], neighbour(0, step)).start()
        to_core(k, [(i, j) for j in (-1, 1) for i in (0, -1, 1, 2)])

    def to_core(k, places):
        for i, j in places:
            ref = piece(k, i, j)
            remote(ref, ref, core_send.at[k], core_recv.at[k], at(x, y, z, 1 - c)).start()

    def stage5(k):
        for side in (0, 1):
            wait_bytes(halves_like(k, side, 4), b_recv.at[k, 2 + side])
        to_core(k, [(i, 2) for i in (0, -1, 1, 2)])

    def stage6(k):
        wait_bytes(core_part(k, 1 - c), core_recv.at[k])

    def exchange(src, dst, index):
        def send(i, carry):
            d = lax.rem(s + i, SEQ)
            remote(src.at[d], dst.at[s], all_send.at[index], all_recv.at[index], (dp, d)).start()
            return carry

        lax.fori_loop(1, SEQ, send, 0)
        dst[pl.ds(s, 1)] = src[pl.ds(s, 1)]

    def arrived(dst, index):
        wait_bytes(dst.at[pl.ds(0, 31)], all_recv.at[index])

    def unpack_pairs():
        for slot in range(5):
            col = (27 + slot) * 128
            for half in range(2):
                block = 2 * slot + half
                for part in range(4):
                    rows = slice(288 * part + 144 * half, 288 * part + 144 * half + 144)
                    target = slice(144 * part, 144 * part + 144)
                    if block == 0:
                        time_out[target, 1024:1152] = wa[rows, col : col + 128]
                    else:
                        cross_out[target, (block - 1) * 128 : block * 128] = wa[rows, col : col + 128]

    def put_rows(recv):
        rows_wide[:, 0:INNER] = recv[...].astype(F32).reshape(ROWS, INNER).astype(BF16)

    order = (R0, R1, RM, RB, R2)
    early = (R0, R1, RM)
    late = (RB, R2)
    wait_bytes(z_recv.at[pl.ds(0, 7), pl.ds(0, 128)], zs_recv.at[0])
    z_wide[:, 0:128, :] = z_recv[:, 0:128, :].astype(F32)

    def spread(k, first):
        base = STAGED[k]
        for j in range(8):
            z_rows[base + 36 * j : base + 36 * j + 36, :] = z_wide[j, first : first + 36, :]
        own[base : base + 288, :] = z_rows[base : base + 288, :].astype(BF16)

    spread(R0, 0)
    stage1(R0)
    spread(R1, 36)
    stage1(R1)
    for j in range(8):
        z_rows[576 + 36 * j : 612 + 36 * j, :] = z_wide[j, 72:108, :]
        z_rows[1296 + 18 * j : 1314 + 18 * j, :] = z_wide[j, 72:90, :]
        z_rows[1440 + 18 * j : 1458 + 18 * j, :] = z_wide[j, 90:108, :]
        z_rows[864 + 18 * j : 882 + 18 * j, :] = z_wide[j, 108:126, :]
    own[576:864, :] = jnp.where(u < 3, z_rows[576:864, :], z_rows[1296:1584, :]).astype(BF16)
    own[864:1008, :] = z_rows[864:1008, :].astype(BF16)
    stage1(RM)
    exchange(latents, latent_recv, 1)
    wait_bytes(z_recv.at[pl.ds(0, 7), pl.ds(128, 48)], zs_recv.at[1])
    z_wide[:, 128:176, :] = z_recv[:, 128:176, :].astype(F32)
    spread(R2, 128)
    for stage in (stage2, stage3, stage4, stage5):
        for k in early:
            stage(k)
    for k in late:
        stage1(k)

    stage6(R0)
    stage6(R1)
    keyval_wide[0:300, :] = dot_nn(caption[...], wa[:, 0:1152])
    keys[0:304, 0:INNER] = keyval_wide[:, 0:INNER].astype(BF16)
    turned = pltpu.roll(keyval_wide[:, 512:1152], 576, 1)
    values[0:304, 0:INNER] = turned[:, 0:INNER].astype(BF16)
    for k in late:
        stage2(k)
    queries[...] = dot_nn(latent_rows[...], wa[:, 1152:1792]).astype(BF16)
    for k in late:
        stage3(k)

    slot = lax.broadcasted_iota(jnp.int32, (1, SLOTS), 1)
    bias = jnp.where(slot < length_ref[0], 0.0, NEG)
    acc[...] = jnp.zeros_like(acc)
    for head in range(HEADS):
        low, high = window(head)
        mask = head_mask(head)
        scores = dot_nt(queries[:, low:high], keys[:, low:high] * mask) * HEAD_SCALE + bias
        weight = jnp.exp(scores - jnp.max(scores, axis=1, keepdims=True))
        soft = weight / jnp.sum(weight, axis=1, keepdims=True)
        probs_c[head] = soft
        acc[:, low:high] += dot_nn(soft.astype(BF16), values[:, low:high] * mask)
    attended = acc[...]
    att_send[...] = attended[:, 0:INNER].reshape(SEQ, 8, INNER).astype(BF16)
    exchange(att_send, att_recv, 4)
    for stage in (stage4, stage5):
        for k in late:
            stage(k)
    stage6(RM)
    unpack_pairs()
    hidden_rows[...] = (
        latent_rows[...].astype(F32) + dot_nn(attended.astype(BF16), cross_out[...])
    ).astype(BF16)
    stage6(RB)
    time_out[0:INNER, 0:1024] = wb[...]
    grad_mixed = dot_nt(grad_branch[...], time_out[...])
    gm_send[...] = grad_mixed[:, 0:INNER].reshape(SEQ, 8, INNER).astype(BF16)
    exchange(gm_send, gm_recv, 0)
    stage6(R2)
    arrived(latent_recv, 1)
    arrived(att_recv, 4)

    put_rows(att_recv)
    latent_patch = latent_recv[...].astype(F32).reshape(ROWS, MODEL)
    rows = (latent_patch + dot_nn(rows_wide[...], cross_out[...])).astype(BF16).astype(F32)
    center = rows - jnp.mean(rows, axis=1, keepdims=True)
    inv_std = lax.rsqrt(jnp.mean(center * center, axis=1, keepdims=True) + EPS)
    normed_ref[...] = center * inv_std
    modded = (normed_ref[...] * scale_row + shift_row).astype(BF16)
    packed = dot_nn(modded, wa[:, 1664:3456])
    packed_ref[0] = pltpu.roll(packed[:, 0:640], 576, 1).astype(BF16)
    packed_ref[1] = packed[:, 640:1280].astype(BF16)
    packed_ref[2] = pltpu.roll(packed[:, 1152:1792], 576, 1).astype(BF16)
    same = (
        lax.broadcasted_iota(jnp.int32, (ROWS, ROWS), 0) % 8 == lax.broadcasted_iota(jnp.int32, (ROWS, ROWS), 1) % 8
    )
    acc[...] = jnp.zeros_like(acc)
    for head in range(HEADS):
        low, high = window(head)
        mask = head_mask(head)
        scores = dot_nt(packed_ref[0, :, low:high], packed_ref[1, :, low:high] * mask) * HEAD_SCALE
        scores = jnp.where(same, scores, NEG)
        weight = jnp.exp(scores - jnp.max(scores, axis=1, keepdims=True))
        soft = weight / jnp.sum(weight, axis=1, keepdims=True)
        probs_t[head] = soft
        acc[:, low:high] += dot_nn(soft.astype(BF16), packed_ref[2, :, low:high] * mask)
    mix_send[...] = acc[:, 0:INNER].reshape(SEQ, 8, INNER).astype(BF16)
    exchange(mix_send, mix_recv, 2)

    arrived(gm_recv, 0)
    put_rows(gm_recv)
    parts = [[None] * 5 for _ in range(3)]

    def add_window(store, low, high, value):
        for block in range(low // 128, high // 128):
            piece_value = value[:, block * 128 - low : block * 128 - low + 128]
            store[block] = piece_value if store[block] is None else store[block] + piece_value

    for head in range(HEADS):
        low, high = window(head)
        mask = head_mask(head)
        soft = probs_t[head]
        grad_head = rows_wide[:, low:high] * mask
        grad_soft = dot_nt(grad_head, packed_ref[2, :, low:high])
        delta = jnp.sum(soft * grad_soft, axis=1, keepdims=True)
        grad_scores = (soft * (grad_soft - delta) * HEAD_SCALE).astype(BF16)
        add_window(parts[0], low, high, dot_nn(grad_scores, packed_ref[1, :, low:high] * mask))
        add_window(parts[1], low, high, dot_tn(grad_scores, packed_ref[0, :, low:high] * mask))
        add_window(parts[2], low, high, dot_tn(soft.astype(BF16), grad_head))
    grad_q, grad_k, grad_v = (jnp.concatenate(store, axis=1) for store in parts)
    grad_q = pltpu.roll(grad_q, 64, 1)
    grad_v = pltpu.roll(grad_v, 64, 1)
    grad_packed = jnp.concatenate(
        [grad_q, grad_k[:, 0:512], grad_k[:, 512:640] + grad_v[:, 0:128], grad_v[:, 128:640]], axis=1
    ).astype(BF16)
    grad_modded = dot_nt(grad_packed, wa[:, 1664:3456])
    mod_sum[0:1, 0:MODEL] = jnp.sum(grad_modded, axis=0, keepdims=True)
    mod_sum[1:2, 0:MODEL] = jnp.sum(grad_modded * normed_ref[...], axis=0, keepdims=True)
    grad_norm = grad_modded * scale_row
    first_mean = jnp.mean(grad_norm, axis=1, keepdims=True)
    second_mean = jnp.mean(grad_norm * normed_ref[...], axis=1, keepdims=True)
    term = inv_std * (grad_norm - first_mean - normed_ref[...] * second_mean)
    term_send[...] = term.reshape(SEQ, 8, MODEL).astype(BF16)
    exchange(term_send, term_recv, 3)

    arrived(mix_recv, 2)
    put_rows(mix_recv)
    mixed = rows_wide[...]
    partial = dot_tn(mixed, grad_branch[...])
    gw_send[...] = partial[0:INNER, :].reshape(72, 8, MODEL).astype(BF16)
    for i in (2, 1, 3, 0):
        part = lax.rem(x + i, 4)
        remote(
            gw_send.at[pl.ds(36 * (1 - c) + 9 * part, 9)],
            gw_core.at[pl.ds(9 * part, 9)],
            red_send.at[0],
            core_part_recv.at[part],
            at(x, y, z, 1 - c),
        ).start()
    branch = dot_nn(mixed, time_out[...])
    out_ref[...] = (hidden_rows[...].astype(F32) + gate_row * branch).astype(BF16)
    mod_sum[2:3, 0:MODEL] = jnp.sum(cotangent[...].astype(F32) * branch, axis=0, keepdims=True)
    for i in range(1, 4):
        remote(mod_sum, mod_y.at[i - 1], red_send.at[6], red_recv.at[6], at(x, y + i, z, c)).start()

    for i in (2, 1, 3, 0):
        part = lax.rem(x + i, 4)
        rows9 = pl.ds(9 * part, 9)
        wait_bytes(gw_core.at[rows9], core_part_recv.at[part])
        gw_half[rows9] = (
            gw_send[pl.ds(36 * c + 9 * part, 9)].astype(F32) + gw_core[rows9].astype(F32)
        ).astype(BF16)
        if i:

            @pl.when(c == 0)
            def _():
                remote(
                    gw_half.at[rows9], gw_x.at[i - 1], red_send.at[1], red_recv.at[1], at(part, y, z, c)
                ).start()

    own_cols = pl.ds(pl.multiple_of(256 * y, 128), 384)
    own_rows = pl.ds(9 * x, 9)

    def total_of(mine, others):
        total = mine.astype(F32)
        for i in range(3):
            total = total + others[i].astype(F32)
        return total.astype(BF16)

    def to_y(source, target, send, recv):
        for i in (2, 1, 3):
            to = lax.rem(y + i, 4)
            cols = pl.ds(pl.multiple_of(256 * to, 128), 384)
            remote(source.at[:, :, cols], target.at[i - 1], send, recv, at(x, to, z, c)).start()

    @pl.when(c == 1)
    def _():
        to_y(gw_half, gw_y1, red_send.at[1], red_recv.at[1])

    wait_bytes(mod_y, red_recv.at[6])
    mod_tile[...] = mod_sum[...] + mod_y[0] + mod_y[1] + mod_y[2]
    for i in range(1, 8):
        to = lax.rem(zl + i, 8)
        block = (36 * (8 * y + to)) // 128
        col = pl.multiple_of(block * 128, 128)
        remote(
            mod_tile.at[:, pl.ds(col, 256)], mod_z.at[i - 1], red_send.at[7], red_recv.at[7], (dp, 8 * y + to)
        ).start()

    @pl.when(c == 0)
    def _():
        wait_bytes(gw_x, red_recv.at[1])
        gw_part[...] = total_of(gw_half[own_rows], gw_x)
        to_y(gw_part, gw_y, red_send.at[2], red_recv.at[2])
        wait_bytes(gw_y, red_recv.at[2])
        gw_tile[...] = total_of(gw_part[:, :, own_cols], gw_y)

    @pl.when(c == 1)
    def _():
        wait_bytes(gw_y1, red_recv.at[1])
        gw_part1[...] = total_of(gw_half[:, :, own_cols], gw_y1)
        for i in (2, 1, 3):
            to = lax.rem(x + i, 4)
            remote(
                gw_part1.at[pl.ds(9 * to, 9)], gw_y.at[i - 1], red_send.at[2], red_recv.at[2], at(to, y, z, c)
            ).start()
        wait_bytes(gw_y, red_recv.at[2])
        gw_tile[...] = total_of(gw_part1[own_rows], gw_y)

    for group in range(9):

        @pl.when(z != group)
        def _():
            remote(
                gw_tile.at[group], gw_z.at[z], red_send.at[3], red_recv.at[3], at(x, y, jnp.int32(group), c)
            ).start()

    arrived(term_recv, 3)
    grad_hidden = (
        cotangent[...].astype(F32) + term_recv[...].astype(F32).reshape(ROWS, MODEL)
    ).astype(BF16)
    grad_attended = dot_nt(grad_hidden, cross_out[...]).astype(BF16)
    acc[...] = jnp.zeros_like(acc)

    def back(head):
        low, high = window(head)
        mask = head_mask(head)
        soft = probs_c[head]
        grad_soft = dot_nt(grad_attended[:, low:high], values[:, low:high] * mask)
        delta = jnp.sum(soft * grad_soft, axis=1, keepdims=True)
        grad_scores = (soft * (grad_soft - delta) * HEAD_SCALE).astype(BF16)
        acc[:, low:high] += dot_nn(grad_scores, keys[:, low:high] * mask)

    @pl.when(z < 9)
    def _():
        wait_bytes(gw_z.at[pl.ds(0, 15)], red_recv.at[3])
        gw_z[pl.ds(z, 1)] = gw_tile[pl.ds(z, 1)]
        total = jnp.sum(gw_z[...].astype(F32), axis=0)
        for place_z in range(8):
            turned = pltpu.roll(total, 384 - (32 * y + 36 * place_z), 1)
            gw_red[place_z] = turned[:, 0:128].astype(BF16)
        gw_all[pl.ds(z, 1)] = gw_red[pl.ds(zl, 1)]

        def send(i, carry):
            remote(
                gw_red.at[lax.rem(zl + i, 8)], gw_all.at[z], red_send.at[4], red_recv.at[4], at(x, y, z + i, c)
            ).start()
            return carry

        lax.fori_loop(1, 16, send, 0)

    for head in range(4):
        back(head)

    @pl.when(z < 9)
    def _():
        wait_bytes(gw_all.at[pl.ds(0, 8)], red_recv.at[4])

    @pl.when(z >= 9)
    def _():
        wait_bytes(gw_all, red_recv.at[4])

    gw_last[pl.ds(u, 1)] = gw_all[...].reshape(1, 9, 8, 128)
    for i in range(1, 8):
        peer = lax.rem(x * 2 + c + i, 8)
        remote(
            gw_all, gw_last.at[u], red_send.at[5], red_recv.at[5], at(peer // 2, y, z, peer % 2)
        ).start()

    for head in range(4, HEADS):
        back(head)
    grad_latents[...] = (
        grad_hidden.astype(F32) + dot_nt(acc[...].astype(BF16), wa[:, 1152:1792])
    ).astype(BF16)

    wait_bytes(mod_z, red_recv.at[7])
    block = (36 * s) // 128
    mod_total = mod_tile[:, pl.ds(pl.multiple_of(block * 128, 128), 256)]
    for i in range(7):
        mod_total = mod_total + mod_z[i]
    mod_total = pltpu.roll(mod_total, lax.rem(256 - (36 * s - 128 * block), 256), 1)
    for i in range(3):
        grad_mod[i] = mod_total[i : i + 1, 0:36] * (SEQ * ROWS) ** (-0.5)

    wait_bytes(gw_last.at[pl.ds(0, 7)], red_recv.at[5])
    total = jnp.transpose(gw_last[...].astype(F32).reshape(INNER, 128))
    grad_weight[...] = total[0:36, :] * (SEQ * ROWS * 16) ** (-0.5)

    wait_bytes(z_recv.at[pl.ds(0, 7), pl.ds(0, 128)], zs_send.at[0])
    wait_bytes(z_recv.at[pl.ds(0, 7), pl.ds(128, 48)], zs_send.at[1])
    for k in order:
        if k == RB:
            wait_bytes(wa.at[pl.ds(0, 144), pl.ds(0, 128 * 15)], ring_send.at[k])
        else:
            wait_bytes(pieces_like(k, 15), ring_send.at[k])
        wait_bytes(core_part(k, c), core_send.at[k])
    for index, ref in ((0, gm_recv), (1, latent_recv), (2, mix_recv), (3, term_recv), (4, att_recv)):
        wait_bytes(ref.at[pl.ds(0, 31)], all_send.at[index])
    wait_bytes(gw_core, red_send.at[0])
    wait_bytes(gw_y, red_send.at[2])

    @pl.when(c == 0)
    def _():
        wait_bytes(gw_x, red_send.at[1])

    @pl.when(c == 1)
    def _():
        wait_bytes(gw_y1, red_send.at[1])


    @pl.when(z < 9)
    def _():
        wait_bytes(gw_z.at[pl.ds(0, 8)], red_send.at[3])
        wait_bytes(gw_z.at[pl.ds(0, 15), :, pl.ds(0, 128)], red_send.at[4])

    @pl.when(z >= 9)
    def _():
        wait_bytes(gw_z.at[pl.ds(0, 9)], red_send.at[3])

    wait_bytes(gw_last.at[pl.ds(0, 7)], red_send.at[5])
    wait_bytes(mod_y, red_send.at[6])
    wait_bytes(mod_z, red_send.at[7])


def body(
    latents,
    caption,
    caption_len,
    modulation,
    cross_query,
    cross_keyval,
    cross_output,
    time_qkv,
    time_output,
    cotangent,
):
    vmem = pl.BlockSpec(memory_space=pltpu.VMEM)
    sems = pltpu.SemaphoreType.DMA
    out, grad_in, grad_mod, grad_w = pl.pallas_call(
        kernel,
        out_shape=(
            jax.ShapeDtypeStruct((ROWS, MODEL), BF16),
            jax.ShapeDtypeStruct((ROWS, MODEL), BF16),
            jax.ShapeDtypeStruct((3, 1, 36), F32),
            jax.ShapeDtypeStruct((36, INNER), F32),
        ),
        in_specs=[vmem] * 7 + [pl.BlockSpec(memory_space=pltpu.SMEM)] + [vmem] * 2,
        out_specs=(vmem,) * 4,
        scratch_shapes=[
            pltpu.VMEM((40, 3456), F32),
            pltpu.VMEM((24, 2304), F32),
            pltpu.VMEM((40, 1792), F32),
            pltpu.VMEM((40, 128), F32),
            pltpu.VMEM((176, 128), F32),
            pltpu.VMEM((176, 128), BF16),
            pltpu.VMEM((8, 176, 128), BF16),
            pltpu.VMEM((8, 176, 128), F32),
            pltpu.VMEM((1584, 128), F32),
            pltpu.VMEM((1296, 128), BF16),
            pltpu.VMEM((304, MODEL), F32),
            pltpu.VMEM((ROWS, MODEL), BF16),
            pltpu.VMEM((ROWS, WIDE), BF16),
            pltpu.VMEM((SEQ, 8, MODEL), BF16),
            pltpu.VMEM((SEQ, 8, INNER), BF16),
            pltpu.VMEM((SEQ, 8, INNER), BF16),
            pltpu.VMEM((MODEL, 4096), BF16),
            pltpu.VMEM((INNER, 1024), BF16),
            pltpu.VMEM((WIDE, MODEL), BF16),
            pltpu.VMEM((WIDE, MODEL), BF16),
            pltpu.VMEM((SLOTS, WIDE), BF16),
            pltpu.VMEM((SLOTS, WIDE), BF16),
            pltpu.VMEM((ROWS, WIDE), BF16),
            pltpu.VMEM((HEADS, ROWS, SLOTS), F32),
            pltpu.VMEM((ROWS, WIDE), F32),
            pltpu.VMEM((ROWS, MODEL), BF16),
            pltpu.VMEM((SEQ, 8, INNER), BF16),
            pltpu.VMEM((SEQ, 8, INNER), BF16),
            pltpu.VMEM((SEQ, 8, INNER), BF16),
            pltpu.VMEM((SEQ, 8, INNER), BF16),
            pltpu.VMEM((SEQ, 8, MODEL), BF16),
            pltpu.VMEM((SEQ, 8, MODEL), BF16),
            pltpu.VMEM((ROWS, MODEL), F32),
            pltpu.VMEM((3, ROWS, WIDE), BF16),
            pltpu.VMEM((HEADS, ROWS, ROWS), F32),
            pltpu.VMEM((ROWS, MODEL), BF16),
            pltpu.VMEM((72, 8, MODEL), BF16),
            pltpu.VMEM((36, 8, MODEL), BF16),
            pltpu.VMEM((36, 8, MODEL), BF16),
            pltpu.VMEM((3, 9, 8, MODEL), BF16),
            pltpu.VMEM((9, 8, MODEL), BF16),
            pltpu.VMEM((3, 36, 8, 384), BF16),
            pltpu.VMEM((36, 8, 384), BF16),
            pltpu.VMEM((3, 9, 8, 384), BF16),
            pltpu.VMEM((9, 8, 384), BF16),
            pltpu.VMEM((16, 8, 384), BF16),
            pltpu.VMEM((8, 8, 128), BF16),
            pltpu.VMEM((9, 8, 128), BF16),
            pltpu.VMEM((8, 9, 8, 128), BF16),
            pltpu.VMEM((8, 1280), F32),
            pltpu.VMEM((3, 8, 1280), F32),
            pltpu.VMEM((8, 1280), F32),
            pltpu.VMEM((7, 8, 256), F32),
            sems((2,)),
            sems((2,)),
            sems((5,)),
            sems((5, 4)),
            sems((5, 4)),
            sems((5,)),
            sems((5,)),
            sems((5,)),
            sems((5,)),
            sems((5,)),
            sems((8,)),
            sems((8,)),
            sems((4,)),
        ],
        compiler_params=pltpu.CompilerParams(
            collective_id=0, has_side_effects=True, vmem_limit_bytes=60 * 2**20
        ),
    )(
        cross_query,
        cross_keyval,
        cross_output,
        time_qkv,
        time_output,
        latents.reshape(SEQ, 8, MODEL),
        caption[0],
        caption_len,
        jnp.swapaxes(modulation, 0, 1),
        cotangent.reshape(ROWS, MODEL),
    )
    return (
        out.reshape(latents.shape),
        grad_in.reshape(latents.shape),
        jnp.swapaxes(grad_mod, 0, 1),
        jnp.swapaxes(grad_w, 0, 1),
    )


def solution(mesh):
    placed = (
        P("dp", "seq", None, None),
        P("dp", None, None),
        P("dp"),
        P("dp", None, None),
        P("seq", None),
        P("seq", None),
        P("seq", None),
        P("seq", None),
        P("seq", None),
        P("dp", "seq", None, None),
    )
    return jax.shard_map(
        body,
        mesh=mesh,
        in_specs=placed,
        out_specs=(
            P("dp", "seq", None, None),
            P("dp", "seq", None, None),
            P("dp", None, "seq"),
            P(None, "seq"),
        ),
        check_vma=False,
    )
```

time: 1960 us -> 165 us (0.08)
  waiting for transfers between devices: 1410 us -> 0 us
  blocking collectives: 336 us -> 0 us
  Pallas kernels: 0 us -> 159 us
  local copies, waits for them, and re-layouts: 69.2 us -> 4.02 us
  starting transfers between devices: 63.4 us -> 0 us
  matrix products: 60.5 us -> 0 us
    all_gather x5 -> x0, waiting for transfers between devices: 1070 us -> none  [the longest x1 232 us: body(): lax.all_gather(time_qkv, 'seq', axis=0, tiled=True)]
    unnamed x2 -> x0, blocking collectives: 336 us -> none
    psum x1 -> x0, waiting for transfers between devices: 318 us -> none  [body(): weight_total = lax.psum(weight_share, 'dp') * total_tokens ** (-0.5)]
    pallas_call x0 -> x1, Pallas kernels: none -> 159 us  [body(): pl.pallas_call(kernel, out_shape=(jax.ShapeDtypeStruct((ROWS, MODEL), BF1...]
    dot_general x18 -> x0, matrix products: 53.7 us -> none  [the longest x1 4.98 us: body(): jnp.dot(modded, qkv_full, preferred_element_type=jnp.float32)]
    all_to_all x4 -> x0, starting transfers between devices: 38.4 us -> none  [relayout(): lax.all_to_all(blocks, 'seq', split_axis=1, concat_axis=0, tiled=True)]
    unnamed x47 -> x10, local copies, waits for them, and re-layouts: 39.7 us -> 4.02 us
    unnamed x8 -> x0, starting transfers between devices: 24.7 us -> none
  transfers between devices with their start and end apart: 18 -> 0, of which waited for: 7 -> 0; matrix products, arithmetic and copies ran while one was open for 10% -> 0% of each run, Pallas kernels for 0% -> 0%
where the time goes in v1:
time: 165 us
  Pallas kernels  159 us (96%)
  local copies, waits for them, and re-layouts  4.02 us (2%)
    pallas_call x1, Pallas kernels, body(): pl.pallas_call(kernel, out_shape=(jax.ShapeDtypeStruct((ROWS, MODEL), BF1...  159 us
    unnamed x10, local copies, waits for them, and re-layouts  4.02 us

profile of v1, /device:TPU:1, one launch (start us, length us, event | category | flops | bytes accessed | tf_op | source)
XLA Modules:
  0.0 164.8 jit_solution(4987243482168370249)
XLA Ops:
  1.3 159.5 %shard_map.129 = (bf16[256,1152]{1,0:T(8,128)(2,1)}, bf16[256,1152]{1,0:T(8,128)(2,1)}, f32[3,1,36]{2,1,0:T(1,128)}, f32[36,576]{1,0:T(8,128)}) custom-call(bf16[36,576]{1,0:T(8,128)(2,1)} %query_shard.1, bf16[36,1152]{1,0:T(8,128)(2,1)} %keyval_shard.1, bf16[18,1152]{1,0:T(8,128)(2,1)} %cross_out_shard.1, bf16[36,1728]{1,0:T(8,128)(2,1)} %qkv_shard.1, ...), custom_call_target="tpu_custom_call" | custom-call | tf_op jit(solution)/shard_map/pallas_call | solution.py:680
  160.8 0.0 copy-start
  160.8 2.0 %copy.19 = bf16[1,1,256,1152]{3,2,1,0:T(8,128)(2,1)} copy(bf16[1,1,256,1152]{3,2,1,0:T(8,128)(2,1)} %bitcast.10) | data formatting | bytes 1179648
  162.7 0.0 copy-done
  162.7 0.0 copy-start.2
  162.8 0.0 copy-start.1
  162.8 0.8 copy.20
  163.6 0.0 copy-done.2
  163.6 0.6 copy.21
  164.1 0.0 copy-done.1
  164.1 0.6 copy.22
Async XLA Ops:
  160.8 2.0 %copy-start = (bf16[256,1152]{1,0:T(8,128)(2,1)S(1)}, bf16[256,1152]{1,0:T(8,128)(2,1)}, u32[]{:S(2)}) copy-start(bf16[256,1152]{1,0:T(8,128)(2,1)} %get-tuple-element.9) | copy-start | bytes 1769476
  162.7 0.8 copy-start.2
  162.8 1.4 copy-start.1

commit v2 on v1

--- a/solution.py
+++ b/solution.py
@@ -296,14 +296,15 @@
     def stage6(k):
         wait_bytes(core_part(k, 1 - c), core_recv.at[k])
 
-    def exchange(src, dst, index):
+    def exchange(src, dst, index, first=1, last=SEQ):
         def send(i, carry):
             d = lax.rem(s + i, SEQ)
             remote(src.at[d], dst.at[s], all_send.at[index], all_recv.at[index], (dp, d)).start()
             return carry
 
-        lax.fori_loop(1, SEQ, send, 0)
-        dst[pl.ds(s, 1)] = src[pl.ds(s, 1)]
+        lax.fori_loop(first, last, send, 0)
+        if first == 1:
+            dst[pl.ds(s, 1)] = src[pl.ds(s, 1)]
 
     def arrived(dst, index):
         wait_bytes(dst.at[pl.ds(0, 31)], all_recv.at[index])
@@ -324,9 +325,9 @@
     def put_rows(recv):
         rows_wide[:, 0:INNER] = recv[...].astype(F32).reshape(ROWS, INNER).astype(BF16)
 
-    order = (R0, R1, RM, RB, R2)
-    early = (R0, R1, RM)
-    late = (RB, R2)
+    order = (RB, RM, R0, R1, R2)
+    early = (RB, RM, R0, R1)
+    late = (R2,)
     wait_bytes(z_recv.at[pl.ds(0, 7), pl.ds(0, 128)], zs_recv.at[0])
     z_wide[:, 0:128, :] = z_recv[:, 0:128, :].astype(F32)
 
@@ -336,10 +337,6 @@
             z_rows[base + 36 * j : base + 36 * j + 36, :] = z_wide[j, first : first + 36, :]
         own[base : base + 288, :] = z_rows[base : base + 288, :].astype(BF16)
 
-    spread(R0, 0)
-    stage1(R0)
-    spread(R1, 36)
-    stage1(R1)
     for j in range(8):
         z_rows[576 + 36 * j : 612 + 36 * j, :] = z_wide[j, 72:108, :]
         z_rows[1296 + 18 * j : 1314 + 18 * j, :] = z_wide[j, 72:90, :]
@@ -347,16 +344,33 @@
         z_rows[864 + 18 * j : 882 + 18 * j, :] = z_wide[j, 108:126, :]
     own[576:864, :] = jnp.where(u < 3, z_rows[576:864, :], z_rows[1296:1584, :]).astype(BF16)
     own[864:1008, :] = z_rows[864:1008, :].astype(BF16)
+    stage1(RB)
     stage1(RM)
-    exchange(latents, latent_recv, 1)
+    spread(R0, 0)
+    stage1(R0)
+    spread(R1, 36)
+    stage1(R1)
+    exchange(latents, latent_recv, 1, 1, 5)
     wait_bytes(z_recv.at[pl.ds(0, 7), pl.ds(128, 48)], zs_recv.at[1])
     z_wide[:, 128:176, :] = z_recv[:, 128:176, :].astype(F32)
     spread(R2, 128)
+    sent = 5
     for stage in (stage2, stage3, stage4, stage5):
         for k in early:
             stage(k)
+            if sent < SEQ:
+                exchange(latents, latent_recv, 1, sent, min(sent + 2, SEQ))
+                sent += 2
     for k in late:
         stage1(k)
+
+    stage6(RB)
+    stage6(RM)
+    unpack_pairs()
+    time_out[0:INNER, 0:1024] = wb[...]
+    grad_mixed = dot_nt(grad_branch[...], time_out[...])
+    gm_send[...] = grad_mixed[:, 0:INNER].reshape(SEQ, 8, INNER).astype(BF16)
+    exchange(gm_send, gm_recv, 0)
 
     stage6(R0)
     stage6(R1)
@@ -387,16 +401,9 @@
     for stage in (stage4, stage5):
         for k in late:
             stage(k)
-    stage6(RM)
-    unpack_pairs()
     hidden_rows[...] = (
         latent_rows[...].astype(F32) + dot_nn(attended.astype(BF16), cross_out[...])
     ).astype(BF16)
-    stage6(RB)
-    time_out[0:INNER, 0:1024] = wb[...]
-    grad_mixed = dot_nt(grad_branch[...], time_out[...])
-    gm_send[...] = grad_mixed[:, 0:INNER].reshape(SEQ, 8, INNER).astype(BF16)
-    exchange(gm_send, gm_recv, 0)
     stage6(R2)
     arrived(latent_recv, 1)
     arrived(att_recv, 4)
@@ -462,9 +469,12 @@
     second_mean = jnp.mean(grad_norm * normed_ref[...], axis=1, keepdims=True)
     term = inv_std * (grad_norm - first_mean - normed_ref[...] * second_mean)
     term_send[...] = term.reshape(SEQ, 8, MODEL).astype(BF16)
-    exchange(term_send, term_recv, 3)
-
     arrived(mix_recv, 2)
+
+    def send_term(first, last):
+        exchange(term_send, term_recv, 3, first, last)
+
+
     put_rows(mix_recv)
     mixed = rows_wide[...]
     partial = dot_tn(mixed, grad_branch[...])
@@ -478,6 +488,7 @@
             core_part_recv.at[part],
             at(x, y, z, 1 - c),
         ).start()
+    send_term(1, 8)
     branch = dot_nn(mixed, time_out[...])
     out_ref[...] = (hidden_rows[...].astype(F32) + gate_row * branch).astype(BF16)
     mod_sum[2:3, 0:MODEL] = jnp.sum(cotangent[...].astype(F32) * branch, axis=0, keepdims=True)
@@ -517,6 +528,8 @@
     @pl.when(c == 1)
     def _():
         to_y(gw_half, gw_y1, red_send.at[1], red_recv.at[1])
+
+    send_term(8, 14)
 
     wait_bytes(mod_y, red_recv.at[6])
     mod_tile[...] = mod_sum[...] + mod_y[0] + mod_y[1] + mod_y[2]
@@ -533,6 +546,7 @@
         wait_bytes(gw_x, red_recv.at[1])
         gw_part[...] = total_of(gw_half[own_rows], gw_x)
         to_y(gw_part, gw_y, red_send.at[2], red_recv.at[2])
+        send_term(14, 20)
         wait_bytes(gw_y, red_recv.at[2])
         gw_tile[...] = total_of(gw_part[:, :, own_cols], gw_y)
 
@@ -545,6 +559,7 @@
             remote(
                 gw_part1.at[pl.ds(9 * to, 9)], gw_y.at[i - 1], red_send.at[2], red_recv.at[2], at(to, y, z, c)
             ).start()
+        send_term(14, 20)
         wait_bytes(gw_y, red_recv.at[2])
         gw_tile[...] = total_of(gw_part1[own_rows], gw_y)
 
@@ -556,6 +571,26 @@
                 gw_tile.at[group], gw_z.at[z], red_send.at[3], red_recv.at[3], at(x, y, jnp.int32(group), c)
             ).start()
 
+    send_term(20, 26)
+    @pl.when(z < 9)
+    def _():
+        wait_bytes(gw_z.at[pl.ds(0, 15)], red_recv.at[3])
+        gw_z[pl.ds(z, 1)] = gw_tile[pl.ds(z, 1)]
+        total = jnp.sum(gw_z[...].astype(F32), axis=0)
+        for place_z in range(8):
+            turned = pltpu.roll(total, 384 - (32 * y + 36 * place_z), 1)
+            gw_red[place_z] = turned[:, 0:128].astype(BF16)
+        gw_all[pl.ds(z, 1)] = gw_red[pl.ds(zl, 1)]
+
+        def send(i, carry):
+            remote(
+                gw_red.at[lax.rem(zl + i, 8)], gw_all.at[z], red_send.at[4], red_recv.at[4], at(x, y, z + i, c)
+            ).start()
+            return carry
+
+        lax.fori_loop(1, 16, send, 0)
+
+    send_term(26, SEQ)
     arrived(term_recv, 3)
     grad_hidden = (
         cotangent[...].astype(F32) + term_recv[...].astype(F32).reshape(ROWS, MODEL)
@@ -571,24 +606,6 @@
         delta = jnp.sum(soft * grad_soft, axis=1, keepdims=True)
         grad_scores = (soft * (grad_soft - delta) * HEAD_SCALE).astype(BF16)
         acc[:, low:high] += dot_nn(grad_scores, keys[:, low:high] * mask)
-
-    @pl.when(z < 9)
-    def _():
-        wait_bytes(gw_z.at[pl.ds(0, 15)], red_recv.at[3])
-        gw_z[pl.ds(z, 1)] = gw_tile[pl.ds(z, 1)]
-        total = jnp.sum(gw_z[...].astype(F32), axis=0)
-        for place_z in range(8):
-            turned = pltpu.roll(total, 384 - (32 * y + 36 * place_z), 1)
-            gw_red[place_z] = turned[:, 0:128].astype(BF16)
-        gw_all[pl.ds(z, 1)] = gw_red[pl.ds(zl, 1)]
-
-        def send(i, carry):
-            remote(
-                gw_red.at[lax.rem(zl + i, 8)], gw_all.at[z], red_send.at[4], red_recv.at[4], at(x, y, z + i, c)
-            ).start()
-            return carry
-
-        lax.fori_loop(1, 16, send, 0)
 
     for head in range(4):
         back(head)

time: 165 us -> 158 us (0.958)
  Pallas kernels: 159 us -> 152 us
    pallas_call x1, Pallas kernels: 159 us -> 152 us  [body(): pl.pallas_call(kernel, out_shape=(jax.ShapeDtypeStruct((ROWS, MODEL), BF1...]
where the time goes in v2:
time: 158 us; the launch traced here: 157 us
  Pallas kernels  152 us (96%)
  local copies, waits for them, and re-layouts  4.02 us (3%)
    pallas_call x1, Pallas kernels, body(): pl.pallas_call(kernel, out_shape=(jax.ShapeDtypeStruct((ROWS, MODEL), BF1...  152 us
    unnamed x10, local copies, waits for them, and re-layouts  4.02 us

profile of v2, /device:TPU:1, one launch (start us, length us, event | category | flops | bytes accessed | tf_op | source)
XLA Modules:
  0.0 156.8 jit_solution(10749575402672389095)
XLA Ops:
  1.3 151.5 %shard_map.129 = (bf16[256,1152]{1,0:T(8,128)(2,1)}, bf16[256,1152]{1,0:T(8,128)(2,1)}, f32[3,1,36]{2,1,0:T(1,128)}, f32[36,576]{1,0:T(8,128)}) custom-call(bf16[36,576]{1,0:T(8,128)(2,1)} %query_shard.1, bf16[36,1152]{1,0:T(8,128)(2,1)} %keyval_shard.1, bf16[18,1152]{1,0:T(8,128)(2,1)} %cross_out_shard.1, bf16[36,1728]{1,0:T(8,128)(2,1)} %qkv_shard.1, ...), custom_call_target="tpu_custom_call" | custom-call | tf_op jit(solution)/shard_map/pallas_call | solution.py:697
  152.8 0.0 copy-start
  152.8 2.0 %copy.19 = bf16[1,1,256,1152]{3,2,1,0:T(8,128)(2,1)} copy(bf16[1,1,256,1152]{3,2,1,0:T(8,128)(2,1)} %bitcast.10) | data formatting | bytes 1179648
  154.8 0.0 copy-done
  154.8 0.0 copy-start.2
  154.8 0.0 copy-start.1
  154.8 0.8 copy.20
  155.6 0.0 copy-done.2
  155.6 0.6 copy.21
  156.2 0.0 copy-done.1
  156.2 0.6 copy.22
Async XLA Ops:
  152.8 2.0 %copy-start = (bf16[256,1152]{1,0:T(8,128)(2,1)S(1)}, bf16[256,1152]{1,0:T(8,128)(2,1)}, u32[]{:S(2)}) copy-start(bf16[256,1152]{1,0:T(8,128)(2,1)} %get-tuple-element.9) | copy-start | bytes 1769476
  154.8 0.8 copy-start.2
  154.8 1.4 copy-start.1

commit v3 on v2

--- a/solution.py
+++ b/solution.py
@@ -469,10 +469,12 @@
     second_mean = jnp.mean(grad_norm * normed_ref[...], axis=1, keepdims=True)
     term = inv_std * (grad_norm - first_mean - normed_ref[...] * second_mean)
     term_send[...] = term.reshape(SEQ, 8, MODEL).astype(BF16)
-    arrived(mix_recv, 2)
 
     def send_term(first, last):
         exchange(term_send, term_recv, 3, first, last)
+
+    send_term(1, 6)
+    arrived(mix_recv, 2)
 
 
     put_rows(mix_recv)
@@ -488,7 +490,7 @@
             core_part_recv.at[part],
             at(x, y, z, 1 - c),
         ).start()
-    send_term(1, 8)
+    send_term(6, 10)
     branch = dot_nn(mixed, time_out[...])
     out_ref[...] = (hidden_rows[...].astype(F32) + gate_row * branch).astype(BF16)
     mod_sum[2:3, 0:MODEL] = jnp.sum(cotangent[...].astype(F32) * branch, axis=0, keepdims=True)
@@ -529,7 +531,7 @@
     def _():
         to_y(gw_half, gw_y1, red_send.at[1], red_recv.at[1])
 
-    send_term(8, 14)
+    send_term(10, 16)
 
     wait_bytes(mod_y, red_recv.at[6])
     mod_tile[...] = mod_sum[...] + mod_y[0] + mod_y[1] + mod_y[2]
@@ -546,7 +548,7 @@
         wait_bytes(gw_x, red_recv.at[1])
         gw_part[...] = total_of(gw_half[own_rows], gw_x)
         to_y(gw_part, gw_y, red_send.at[2], red_recv.at[2])
-        send_term(14, 20)
+        send_term(16, 21)
         wait_bytes(gw_y, red_recv.at[2])
         gw_tile[...] = total_of(gw_part[:, :, own_cols], gw_y)
 
@@ -559,7 +561,7 @@
             remote(
                 gw_part1.at[pl.ds(9 * to, 9)], gw_y.at[i - 1], red_send.at[2], red_recv.at[2], at(to, y, z, c)
             ).start()
-        send_term(14, 20)
+        send_term(16, 21)
         wait_bytes(gw_y, red_recv.at[2])
         gw_tile[...] = total_of(gw_part1[own_rows], gw_y)
 
@@ -571,7 +573,7 @@
                 gw_tile.at[group], gw_z.at[z], red_send.at[3], red_recv.at[3], at(x, y, jnp.int32(group), c)
             ).start()
 
-    send_term(20, 26)
+    send_term(21, 26)
     @pl.when(z < 9)
     def _():
         wait_bytes(gw_z.at[pl.ds(0, 15)], red_recv.at[3])

time: 158 us -> 161 us (1.019)
  Pallas kernels: 152 us -> 155 us
    pallas_call x1, Pallas kernels: 152 us -> 155 us  [body(): pl.pallas_call(kernel, out_shape=(jax.ShapeDtypeStruct((ROWS, MODEL), BF1...]
where the time goes in v3:
time: 161 us
  Pallas kernels  155 us (96%)
  local copies, waits for them, and re-layouts  4.02 us (2%)
    pallas_call x1, Pallas kernels, body(): pl.pallas_call(kernel, out_shape=(jax.ShapeDtypeStruct((ROWS, MODEL), BF1...  155 us
    unnamed x10, local copies, waits for them, and re-layouts  4.02 us

profile of v3, /device:TPU:1, one launch (start us, length us, event | category | flops | bytes accessed | tf_op | source)
XLA Modules:
  0.0 160.7 jit_solution(17074370897371297968)
XLA Ops:
  1.3 155.4 %shard_map.129 = (bf16[256,1152]{1,0:T(8,128)(2,1)}, bf16[256,1152]{1,0:T(8,128)(2,1)}, f32[3,1,36]{2,1,0:T(1,128)}, f32[36,576]{1,0:T(8,128)}) custom-call(bf16[36,576]{1,0:T(8,128)(2,1)} %query_shard.1, bf16[36,1152]{1,0:T(8,128)(2,1)} %keyval_shard.1, bf16[18,1152]{1,0:T(8,128)(2,1)} %cross_out_shard.1, bf16[36,1728]{1,0:T(8,128)(2,1)} %qkv_shard.1, ...), custom_call_target="tpu_custom_call" | custom-call | tf_op jit(solution)/shard_map/pallas_call | solution.py:699
  156.7 0.0 copy-start
  156.7 2.0 %copy.19 = bf16[1,1,256,1152]{3,2,1,0:T(8,128)(2,1)} copy(bf16[1,1,256,1152]{3,2,1,0:T(8,128)(2,1)} %bitcast.10) | data formatting | bytes 1179648
  158.7 0.0 copy-done
  158.7 0.0 copy-start.2
  158.7 0.0 copy-start.1
  158.7 0.8 copy.20
  159.5 0.0 copy-done.2
  159.5 0.6 copy.21
  160.1 0.0 copy-done.1
  160.1 0.6 copy.22
Async XLA Ops:
  156.7 2.0 %copy-start = (bf16[256,1152]{1,0:T(8,128)(2,1)S(1)}, bf16[256,1152]{1,0:T(8,128)(2,1)}, u32[]{:S(2)}) copy-start(bf16[256,1152]{1,0:T(8,128)(2,1)} %get-tuple-element.9) | copy-start | bytes 1769476
  158.7 0.8 copy-start.2
  158.7 1.4 copy-start.1
